TPU v7x, 32 devices: a whole 2x2x4 slice. The times are simulated.
32 devices in a mesh: track: 4 (over x, core), tm: 8 (over z, y).
Axes of the slice: x: 2, y: 2, z: 4, core: 2. Of those that a mesh axis runs over, the one named last changes fastest.
Arguments:
- diffusion_latents: bfloat16 [8, 512, 64], P(None, 'tm', 'track'), may hold values from -6 to 6
- lengths: int32 [8], P('track'), may hold values from 64 to 512, as said below
- input_conv_weight: bfloat16 [7, 64, 1024], replicated, may hold values from -0.25 to 0.25
- upsample_snake_params: float32 [2, 1024], replicated, may hold values from 0.5 to 2
- transposed_conv_weight: bfloat16 [1024, 16, 512], replicated, may hold values from -0.125 to 0.125
- residual_snake_params: float32 [2, 2, 2, 512], replicated, may hold values from 0.5 to 2
- residual_dilated_weight: bfloat16 [2, 7, 512, 512], replicated, may hold values from -0.09375 to 0.09375
- residual_pointwise_weight: bfloat16 [2, 512, 512], replicated, may hold values from -0.25 to 0.25
Outputs:
- decoded: bfloat16 [8, 4096, 512], P('track', 'tm')
Inputs may be any that keep to these rules, and one draw needn't show every extreme that they name: `lengths`: every draw has at least one track of all 512 frames.
All inputs are finite; a program needn't handle non-finite values.
Results may differ from a plain program's by a relative error of at most 0.03.
Values may be sent and summed in bfloat16 or wider, within the bound.
A program may use at most 128 MiB of HBM per device.

v0:
```python
import functools
import math

import jax
import jax.numpy as jnp
from jax import lax
from jax.experimental import pallas as pl
from jax.experimental.pallas import tpu as pltpu
from jax.sharding import PartitionSpec as P

MESH = pl.DeviceIdType.MESH
LEAD = 4
CHUNK = 64
GROUP = 2
SIN2 = (9.86952174, -32.4650355, 42.6422709, -29.4210797, 10.573119)


def snake(value, turn, gain):
    turns = value * turn
    rest = turns - jnp.round(turns)
    square = rest * rest
    wave = SIN2[-1]
    for factor in SIN2[-2::-1]:
        wave = wave * square + factor
    return value + (wave * square) * gain


def live_rows(row, per_track, base, lead, lens):
    second = row >= per_track
    frame = base - lead + row - jnp.where(second, per_track, 0)
    limit = jnp.where(second, lens[1], lens[0])
    return (frame >= 0) & (frame < limit)


def kernel(
    track_count,
    time_count,
    lens_ref,
    x_ref,
    up_ref,
    res_ref,
    wi_hbm,
    wt_hbm,
    wd_hbm,
    wp_hbm,
    out_ref,
    recv,
    wi,
    raw,
    table,
    wd,
    wp,
    columns,
    shaped,
    sig0,
    sig1,
    act0,
    act1,
    final,
    send_sem,
    recv_sem,
    own_sem,
    wi_sem,
    raw_sem,
    wd_sem,
    wp_sem,
):
    frames = x_ref.shape[2]
    rows = shaped.shape[1]
    per_track = rows // 2
    stride = sig0.shape[0]
    half = stride // 2
    width = sig0.shape[2]
    wide = table.shape[1] // 2
    part = x_ref.shape[1]
    taps = wd.shape[1]
    t = lax.axis_index("track")
    m = lax.axis_index("tm")
    base = m * frames

    chunks = raw.shape[0]
    wi_copy = pltpu.make_async_copy(wi_hbm, wi.at[pl.ds(0, wi_hbm.shape[0])], wi_sem)
    wi_copy.start()
    raw_copies = [
        pltpu.make_async_copy(wt_hbm.at[pl.ds(i * CHUNK, CHUNK)], raw.at[i], raw_sem.at[i])
        for i in range(chunks)
    ]
    for copy in raw_copies:
        copy.start()
    wd_copies = [pltpu.make_async_copy(wd_hbm.at[u], wd.at[u], wd_sem.at[u]) for u in range(2)]
    wp_copy = pltpu.make_async_copy(wp_hbm, wp, wp_sem)
    wd_copies[0].start()
    wp_copy.start()
    wd_copies[1].start()

    peers = []
    for o in range(3):
        for i in range(track_count):
            if o == 1 and i == 0:
                continue
            peers.append((o, i))
    barrier = pltpu.get_barrier_semaphore()

    def place(o, i):
        return {
            "track": lax.rem(t + i, track_count),
            "tm": lax.rem(m + o - 1 + time_count, time_count),
        }

    for o, i in peers:
        pl.semaphore_signal(barrier, inc=1, device_id=place(o, i), device_id_type=MESH)
    pl.semaphore_wait(barrier, len(peers))
    own = pltpu.make_async_copy(x_ref.at[pl.ds(2 * t, 2)], recv.at[1, t], own_sem)
    own.start()
    sends = []
    for o, i in peers:
        target = place(o, i)
        copy = pltpu.make_async_remote_copy(
            src_ref=x_ref.at[pl.ds(2 * target["track"], 2)],
            dst_ref=recv.at[2 - o, t],
            send_sem=send_sem.at[o, i],
            recv_sem=recv_sem.at[o, i],
            device_id=target,
            device_id_type=MESH,
        )
        copy.start()
        sends.append(copy)

    wi[pl.ds(wi_hbm.shape[0], wi.shape[0] - wi_hbm.shape[0])] = jnp.zeros(
        (wi.shape[0] - wi_hbm.shape[0], wide), jnp.bfloat16
    )

    @pl.loop(0, chunks)
    def _(i):
        pltpu.make_async_copy(
            wt_hbm.at[pl.ds(i * CHUNK, CHUNK)], raw.at[i], raw_sem.at[i]
        ).wait()
        for h in range(CHUNK // 16):
            piece = jnp.swapaxes(raw[i, h * 16 : h * 16 + 16], 0, 1)
            place_at = pl.multiple_of(i * CHUNK + h * 16, 16)
            for tap in range(2 * stride):
                if half <= tap < half + stride:
                    table[tap - half, pl.ds(place_at, 16)] = piece[tap]
                else:
                    phase = (tap + half) % stride if tap < half else tap - stride - half
                    table[phase, pl.ds(wide + place_at, 16)] = piece[tap]

    own.wait()
    for copy in sends:
        copy.wait()
    wi_copy.wait()

    lens = (lens_ref[0], lens_ref[1])
    lane = lax.broadcasted_iota(jnp.int32, (1, 128), 1)
    edge = (128 - frames) // 2
    for track in range(2):
        def slab(o):
            piece = recv[o, :, track].reshape(track_count * part, frames).astype(jnp.float32)
            return jnp.concatenate(
                [piece, jnp.zeros((track_count * part, 128 - frames), jnp.float32)], axis=1
            )

        low = pltpu.roll(slab(0), 128 + edge - frames, 1)
        mid = pltpu.roll(slab(1), edge, 1)
        high = pltpu.roll(slab(2), edge + frames, 1)
        joined = jnp.where(lane < edge, low, jnp.where(lane < edge + frames, mid, high))
        place_of = base + lane - edge
        joined = jnp.where((place_of >= 0) & (place_of < lens[track]), joined, 0.0)
        stacked = [
            pltpu.roll(joined, 128 - (k - taps // 2 + edge - LEAD), 1) for k in range(taps)
        ]
        missing = wi.shape[0] - taps * track_count * part
        stacked.append(jnp.zeros((missing, 128), jnp.float32))
        block = jnp.concatenate(stacked, axis=0).T
        columns[pl.ds(track * per_track, per_track)] = block[:per_track]

    row = lax.broadcasted_iota(jnp.int32, (rows, 1), 0)
    live = live_rows(row, per_track, base, LEAD, lens)
    lhs = columns[...].astype(jnp.bfloat16)
    for n in range(0, wide, 256):
        hidden = jnp.dot(lhs, wi[:, n : n + 256], preferred_element_type=jnp.float32)
        hidden = jnp.where(live, hidden, 0.0).astype(jnp.bfloat16).astype(jnp.float32)
        turn = up_ref[0:1, n : n + 256] * (1.0 / math.pi)
        value = snake(hidden, turn, 1.0 / up_ref[1:2, n : n + 256])
        plain = value.astype(jnp.bfloat16)
        shaped[0, :, n : n + 256] = plain
        shaped[1, :, n : n + 256] = plain
        shaped[0, :, wide + n : wide + n + 256] = pltpu.roll(value, 1, 0).astype(jnp.bfloat16)
        shaped[1, :, wide + n : wide + n + 256] = pltpu.roll(value, rows - 1, 0).astype(jnp.bfloat16)

    def coefficients(u, i):
        return res_ref[u, i, 0:1] * (1.0 / math.pi), 1.0 / res_ref[u, i, 1:2]

    first = coefficients(0, 0)

    @pl.loop(0, stride)
    def _(p):
        summed = jnp.dot(shaped[p // half], table[p], preferred_element_type=jnp.float32)
        signal = jnp.where(live, summed, 0.0).astype(jnp.bfloat16)
        sig0[p] = signal
        value = snake(signal.astype(jnp.float32), *first)
        act0[p + 3] = value.astype(jnp.bfloat16)

        @pl.when(p <= 2)
        def _():
            act0[p + 11] = pltpu.roll(value, rows - 1, 0).astype(jnp.bfloat16)

        @pl.when(p >= stride - 3)
        def _():
            act0[p - 5] = pltpu.roll(value, 1, 0).astype(jnp.bfloat16)

    wd_copies[0].wait()
    wp_copy.wait()
    second = coefficients(0, 1)
    third = coefficients(1, 0)

    def inner(value, shift):
        moved = pltpu.roll(value, rows - (LEAD + shift), 0)
        return jnp.concatenate([moved[:frames], moved[per_track : per_track + frames]], axis=0)

    @pl.loop(0, stride // GROUP)
    def _(step):
        p0 = step * GROUP
        summed = jnp.zeros((GROUP * rows, width), jnp.float32)
        for k in range(taps):
            window = act0[pl.ds(p0 + k, GROUP)].reshape(GROUP * rows, width)
            summed = summed + jnp.dot(window, wd[0, k], preferred_element_type=jnp.float32)
        pointed = snake(summed, *second).astype(jnp.bfloat16)
        branch = jnp.dot(pointed, wp[0], preferred_element_type=jnp.float32)
        for j in range(GROUP):
            p = p0 + j
            total = sig0[p].astype(jnp.float32) + branch[j * rows : (j + 1) * rows]
            signal = jnp.where(live, total, 0.0).astype(jnp.bfloat16).astype(jnp.float32)
            sig1[p] = inner(signal, 0).astype(jnp.bfloat16)
            value = snake(signal, *third)
            act1[p + 9] = inner(value, 0).astype(jnp.bfloat16)
            act1[p + 17] = inner(value, 1).astype(jnp.bfloat16)
            act1[p + 1] = inner(value, -1).astype(jnp.bfloat16)

            @pl.when(p == 0)
            def _():
                act1[25] = inner(value, 2).astype(jnp.bfloat16)

            @pl.when(p == stride - 1)
            def _():
                act1[0] = inner(value, -2).astype(jnp.bfloat16)

    wd_copies[1].wait()
    fourth = coefficients(1, 1)
    core = 2 * frames
    core_row = lax.broadcasted_iota(jnp.int32, (core, 1), 0)
    core_live = live_rows(core_row, frames, base, 0, lens)

    @pl.loop(0, stride // GROUP)
    def _(step):
        p0 = step * GROUP
        summed = jnp.zeros((GROUP * core, width), jnp.float32)
        for k in range(taps):
            window = act1[pl.ds(p0 + 3 * k, GROUP)].reshape(GROUP * core, width)
            summed = summed + jnp.dot(window, wd[1, k], preferred_element_type=jnp.float32)
        pointed = snake(summed, *fourth).astype(jnp.bfloat16)
        branch = jnp.dot(pointed, wp[1], preferred_element_type=jnp.float32)
        for j in range(GROUP):
            total = sig1[p0 + j].astype(jnp.float32) + branch[j * core : (j + 1) * core]
            final[p0 + j] = jnp.where(core_live, total, 0.0)

    for track in range(2):
        for c in range(frames // 16):
            block = jnp.swapaxes(final[:, track * frames + c * 16 : track * frames + c * 16 + 16], 0, 1)
            out_ref[track, c * 16 * stride : (c + 1) * 16 * stride] = block.reshape(
                16 * stride, width
            ).astype(jnp.bfloat16)


def local(mesh, latents, lengths, w_in, up_params, w_up, res_params, w_dil, w_point):
    track_count, time_count = mesh.shape["track"], mesh.shape["tm"]
    part_tracks, frames, part = latents.shape[0] // track_count, latents.shape[1], latents.shape[2]
    taps, _, wide = w_in.shape
    stride, width = w_up.shape[1] // 2, w_up.shape[2]
    rows = 2 * (frames + 2 * LEAD)
    depth = -(-taps * track_count * part // 128) * 128
    chunks = wide // CHUNK
    bf = jnp.bfloat16
    vmem = pl.BlockSpec(memory_space=pltpu.VMEM)
    hbm = pl.BlockSpec(memory_space=pl.ANY)
    return pl.pallas_call(
        functools.partial(kernel, track_count, time_count),
        out_shape=jax.ShapeDtypeStruct((part_tracks, frames * stride, width), bf),
        in_specs=[pl.BlockSpec(memory_space=pltpu.SMEM), vmem, vmem, vmem, hbm, hbm, hbm, hbm],
        out_specs=vmem,
        scratch_shapes=[
            pltpu.VMEM((3, track_count, 2, part, frames), bf),
            pltpu.VMEM((depth, wide), bf),
            pltpu.VMEM((chunks, CHUNK, 2 * stride, width), bf),
            pltpu.VMEM((stride, 2 * wide, width), bf),
            pltpu.VMEM(w_dil.shape, bf),
            pltpu.VMEM(w_point.shape, bf),
            pltpu.VMEM((rows, depth), jnp.float32),
            pltpu.VMEM((2, rows, 2 * wide), bf),
            pltpu.VMEM((stride, rows, width), bf),
            pltpu.VMEM((stride, 2 * frames, width), bf),
            pltpu.VMEM((stride + 6, rows, width), bf),
            pltpu.VMEM((stride + 18, 2 * frames, width), bf),
            pltpu.VMEM((stride, 2 * frames, width), jnp.float32),
            pltpu.SemaphoreType.DMA((3, track_count)),
            pltpu.SemaphoreType.DMA((3, track_count)),
            pltpu.SemaphoreType.DMA,
            pltpu.SemaphoreType.DMA,
            pltpu.SemaphoreType.DMA((chunks,)),
            pltpu.SemaphoreType.DMA((2,)),
            pltpu.SemaphoreType.DMA,
        ],
        compiler_params=pltpu.CompilerParams(
            collective_id=0, has_side_effects=True, vmem_limit_bytes=63 * 2**20
        ),
        name="decoder",
    )(
        lengths,
        jnp.transpose(latents, (0, 2, 1)),
        up_params,
        res_params,
        w_in.reshape(taps * w_in.shape[1], wide),
        w_up,
        w_dil,
        w_point,
    )


def solution(mesh):
    in_specs = (P(None, "tm", "track"), P("track"), P(), P(), P(), P(), P(), P())
    out_specs = P("track", "tm", None)
    return jax.shard_map(
        functools.partial(local, mesh),
        mesh=mesh,
        in_specs=in_specs,
        out_specs=out_specs,
        check_vma=False,
    )
```

profile of v0, /device:TPU:0, one launch (start us, length us, event | category | flops | bytes accessed | tf_op | source)
XLA Modules:
  0.0 37.1 jit_solution(10577504566994283435)
XLA Ops:
  0.0 34.8 %decoder.1 = bf16[2,512,512]{2,1,0:T(8,128)(2,1)} custom-call(s32[2]{0:T(128)} %lens_ref.1, bf16[8,16,64]{2,1,0:T(8,128)(2,1)} %bitcast.3, f32[2,1024]{1,0:T(2,128)} %up_ref.1, f32[2,2,2,512]{3,2,1,0:T(2,128)} %res_ref.1, bf16[448,1024]{1,0:T(8,128)(2,1)} %bitcast.2, bf16[1024,16,512]{2,1,0:T(8,128)(2,1)} %wt_hbm.1, bf16[2,7,512,512]{3,2,1,0:T(8,128)(2,1)} %wd_hbm.1, ...), custom_call_target="tpu_custom_call" | custom-call | tf_op jit(solution)/shard_map/decoder/pallas_call | solution.py:286
  34.8 2.3 %copy.10 = bf16[2,512,512]{2,1,0:T(8,128)(2,1)} copy(bf16[2,512,512]{2,1,0:T(8,128)(2,1)} %decoder.1) | data formatting | bytes 2097152
where the time goes:
time: 37.3 us; the launch traced here: 37.1 us
  Pallas kernels  34.8 us (93%)
  local copies, waits for them, and re-layouts  2.26 us (6%)
    pallas_call x1, Pallas kernels, local(): pl.pallas_call(functools.partial(kernel, track_count, time_count), out_sh...  34.8 us
    unnamed x1, local copies, waits for them, and re-layouts  2.26 us

commit v1 on v0

--- a/solution.py
+++ b/solution.py
@@ -104,12 +104,24 @@
     def place(o, i):
         return {
             "track": lax.rem(t + i, track_count),
-            "tm": lax.rem(m + o - 1 + time_count, time_count),
+            "tm": m + o - 1,
         }
 
+    inside = {0: m > 0, 1: None, 2: m < time_count - 1}
+
+    def guarded(o, action):
+        if inside[o] is None:
+            action()
+        else:
+            pl.when(inside[o])(action)
+
+    def greet(o, i):
+        pl.semaphore_signal(barrier, inc=1, device_id=place(o, i), device_id_type=MESH)
+
     for o, i in peers:
-        pl.semaphore_signal(barrier, inc=1, device_id=place(o, i), device_id_type=MESH)
-    pl.semaphore_wait(barrier, len(peers))
+        guarded(o, functools.partial(greet, o, i))
+    sides = jnp.where(m > 0, 1, 0) + jnp.where(m < time_count - 1, 1, 0)
+    pl.semaphore_wait(barrier, track_count - 1 + track_count * sides)
     own = pltpu.make_async_copy(x_ref.at[pl.ds(2 * t, 2)], recv.at[1, t], own_sem)
     own.start()
     sends = []
@@ -123,8 +135,8 @@
             device_id=target,
             device_id_type=MESH,
         )
-        copy.start()
-        sends.append(copy)
+        guarded(o, copy.start)
+        sends.append((o, copy))
 
     wi[pl.ds(wi_hbm.shape[0], wi.shape[0] - wi_hbm.shape[0])] = jnp.zeros(
         (wi.shape[0] - wi_hbm.shape[0], wide), jnp.bfloat16
@@ -146,8 +158,9 @@
                     table[phase, pl.ds(wide + place_at, 16)] = piece[tap]
 
     own.wait()
-    for copy in sends:
-        copy.wait()
+    for o, copy in sends:
+        guarded(o, copy.wait_send)
+        guarded(2 - o, copy.wait_recv)
     wi_copy.wait()
 
     lens = (lens_ref[0], lens_ref[1])

time: 37.3 us -> 34.2 us (0.917)
  Pallas kernels: 34.8 us -> 31.7 us
    pallas_call x1, Pallas kernels: 34.8 us -> 31.7 us  [local(): pl.pallas_call(functools.partial(kernel, track_count, time_count), out_sh...]
where the time goes in v1:
time: 34.2 us; the launch traced here: 33.9 us
  Pallas kernels  31.7 us (93%)
  local copies, waits for them, and re-layouts  2.26 us (7%)
    pallas_call x1, Pallas kernels, local(): pl.pallas_call(functools.partial(kernel, track_count, time_count), out_sh...  31.7 us
    unnamed x1, local copies, waits for them, and re-layouts  2.26 us

profile of v1, /device:TPU:0, one launch (start us, length us, event | category | flops | bytes accessed | tf_op | source)
XLA Modules:
  0.0 33.9 jit_solution(1137587180251808371)
XLA Ops:
  0.0 31.7 %decoder.1 = bf16[2,512,512]{2,1,0:T(8,128)(2,1)} custom-call(s32[2]{0:T(128)} %lens_ref.1, bf16[8,16,64]{2,1,0:T(8,128)(2,1)} %bitcast.3, f32[2,1024]{1,0:T(2,128)} %up_ref.1, f32[2,2,2,512]{3,2,1,0:T(2,128)} %res_ref.1, bf16[448,1024]{1,0:T(8,128)(2,1)} %bitcast.2, bf16[1024,16,512]{2,1,0:T(8,128)(2,1)} %wt_hbm.1, bf16[2,7,512,512]{3,2,1,0:T(8,128)(2,1)} %wd_hbm.1, ...), custom_call_target="tpu_custom_call" | custom-call | tf_op jit(solution)/shard_map/decoder/pallas_call | solution.py:299
  31.7 2.3 %copy.10 = bf16[2,512,512]{2,1,0:T(8,128)(2,1)} copy(bf16[2,512,512]{2,1,0:T(8,128)(2,1)} %decoder.1) | data formatting | bytes 2097152

commit v2 on v1

--- a/solution.py
+++ b/solution.py
@@ -206,7 +206,7 @@
 
     first = coefficients(0, 0)
 
-    @pl.loop(0, stride)
+    @pl.loop(0, stride, unroll=True)
     def _(p):
         summed = jnp.dot(shaped[p // half], table[p], preferred_element_type=jnp.float32)
         signal = jnp.where(live, summed, 0.0).astype(jnp.bfloat16)
@@ -231,7 +231,7 @@
         moved = pltpu.roll(value, rows - (LEAD + shift), 0)
         return jnp.concatenate([moved[:frames], moved[per_track : per_track + frames]], axis=0)
 
-    @pl.loop(0, stride // GROUP)
+    @pl.loop(0, stride // GROUP, unroll=True)
     def _(step):
         p0 = step * GROUP
         summed = jnp.zeros((GROUP * rows, width), jnp.float32)
@@ -264,7 +264,7 @@
     core_row = lax.broadcasted_iota(jnp.int32, (core, 1), 0)
     core_live = live_rows(core_row, frames, base, 0, lens)
 
-    @pl.loop(0, stride // GROUP)
+    @pl.loop(0, stride // GROUP, unroll=True)
     def _(step):
         p0 = step * GROUP
         summed = jnp.zeros((GROUP * core, width), jnp.float32)

time: 34.2 us -> 31 us (0.906)
  Pallas kernels: 31.7 us -> 28.5 us
    pallas_call x1, Pallas kernels: 31.7 us -> 28.5 us  [local(): pl.pallas_call(functools.partial(kernel, track_count, time_count), out_sh...]
where the time goes in v2:
time: 31 us; the launch traced here: 30.7 us
  Pallas kernels  28.5 us (92%)
  local copies, waits for them, and re-layouts  2.26 us (7%)
    pallas_call x1, Pallas kernels, local(): pl.pallas_call(functools.partial(kernel, track_count, time_count), out_sh...  28.5 us
    unnamed x1, local copies, waits for them, and re-layouts  2.26 us

profile of v2, /device:TPU:0, one launch (start us, length us, event | category | flops | bytes accessed | tf_op | source)
XLA Modules:
  0.0 30.7 jit_solution(9542205312059660737)
XLA Ops:
  0.0 28.5 %decoder.1 = bf16[2,512,512]{2,1,0:T(8,128)(2,1)} custom-call(s32[2]{0:T(128)} %lens_ref.1, bf16[8,16,64]{2,1,0:T(8,128)(2,1)} %bitcast.3, f32[2,1024]{1,0:T(2,128)} %up_ref.1, f32[2,2,2,512]{3,2,1,0:T(2,128)} %res_ref.1, bf16[448,1024]{1,0:T(8,128)(2,1)} %bitcast.2, bf16[1024,16,512]{2,1,0:T(8,128)(2,1)} %wt_hbm.1, bf16[2,7,512,512]{3,2,1,0:T(8,128)(2,1)} %wd_hbm.1, ...), custom_call_target="tpu_custom_call" | custom-call | tf_op jit(solution)/shard_map/decoder/pallas_call | solution.py:299
  28.5 2.3 %copy.10 = bf16[2,512,512]{2,1,0:T(8,128)(2,1)} copy(bf16[2,512,512]{2,1,0:T(8,128)(2,1)} %decoder.1) | data formatting | bytes 2097152
